TPU v7x, 32 devices: a whole 2x2x4 slice. The times are simulated.
32 devices in a mesh: head: 4 (over x, core), seq: 8 (over z, y).
Axes of the slice: x: 2, y: 2, z: 4, core: 2. Of those that a mesh axis runs over, the one named last changes fastest.
Arguments:
- x_input: bfloat16 [8192, 16384], P('seq', 'head'), may hold values from -5 to 5
- bc_input: bfloat16 [2, 8192, 1024], P(None, 'seq', 'head'), may hold values from -5 to 5
- dt_input: bfloat16 [8192, 128], P('seq', 'head'), may hold values from -8 to 256
- z_gate: bfloat16 [8192, 16384], P('seq', 'head'), may hold values from -400 to 400
- conv_x: float32 [4, 16384], P(None, 'head'), may hold values from -2 to 2
- conv_bc: float32 [2, 4, 1024], P(None, None, 'head'), may hold values from -2 to 2
- dt_bias: float32 [128], P('head'), may hold values from -0.3 to 0.3
- a_log: float32 [128], P('head'), may hold values from -10 to 1
- d_skip: float32 [128], P('head'), may hold values from 0.5 to 1.5
- init_state: float32 [128, 128, 128], P('head'), may hold values from -5 to 5
- norm_gain: float32 [16384], P('head'), may hold values from 0.5 to 1.5
Outputs:
- normed: bfloat16 [8192, 16384], P('seq', 'head')
All inputs are finite; a program needn't handle non-finite values.
Results may differ from a plain program's by a relative error of at most 0.0034.
Values may be sent and summed in bfloat16 or wider, within the bound.
A program may use at most 128 MiB of HBM per device.

v0:
```python
import jax
import jax.numpy as jnp
from jax import lax
from jax.sharding import PartitionSpec as P

SPAN = 256
INNER = 16384
norm_eps = 1e-05


def from_behind(value, axis, by):
    length = lax.axis_size(axis)
    pairs = [(i, i + by) for i in range(length) if 0 <= i + by < length]
    return lax.ppermute(value, axis, pairs)


def combine_states(earlier, later):
    return (earlier[0] * later[0], later[0][..., None, None] * earlier[1] + later[1])


def prefix_sources(pieces):
    inclusive = lax.associative_scan(combine_states, pieces, axis=0)
    return jnp.concatenate([jnp.zeros_like(pieces[1][:1]), inclusive[1][:-1]], axis=0)


def local(
    x_input,
    bc_input,
    dt_input,
    z_gate,
    conv_x,
    conv_bc,
    dt_bias,
    a_log,
    d_skip,
    init_state,
    norm_gain,
):
    row_count = x_input.shape[0]
    channels = x_input.shape[1]
    heads_here = a_log.shape[0]
    head_dim = init_state.shape[1]
    state_dim = init_state.shape[2]
    groups_here = bc_input.shape[2] // state_dim
    group_heads = heads_here // groups_here
    segment_len = SPAN
    segments = row_count // segment_len
    rim_rows = conv_x.shape[0] - 1
    x_rim, bc_rim = from_behind(
        (x_input[row_count - rim_rows :], bc_input[:, row_count - rim_rows :]), "seq", 1
    )
    x_full = jnp.concatenate([x_rim, x_input], axis=0)
    bc_full = jnp.concatenate([bc_rim, bc_input], axis=1)
    x_sum = jnp.zeros((row_count, channels), jnp.float32)
    bc_sum = jnp.zeros(bc_input.shape, jnp.float32)
    for tap_index in range(rim_rows + 1):
        x_sum = x_sum + conv_x[tap_index] * x_full[tap_index : tap_index + row_count]
        bc_sum = (
            bc_sum
            + conv_bc[:, tap_index][:, None, :] * bc_full[:, tap_index : tap_index + row_count]
        )
    x_conv = jax.nn.silu(x_sum).astype(jnp.bfloat16)
    bc_conv = jax.nn.silu(bc_sum).astype(jnp.bfloat16)
    b_mat = bc_conv[0].reshape(segments, segment_len, groups_here, state_dim)
    c_mat = bc_conv[1].reshape(segments, segment_len, groups_here, state_dim)
    time_step = jax.nn.softplus(dt_input.astype(jnp.float32) + dt_bias).reshape(
        segments, segment_len, heads_here
    )
    log_cum = jnp.cumsum(-jnp.exp(a_log) * time_step, axis=1)
    scores = jnp.einsum("clgn,csgn->cgls", c_mat, b_mat, preferred_element_type=jnp.float32)
    cum_heads = jnp.transpose(log_cum, (0, 2, 1))
    step_heads = jnp.transpose(time_step, (0, 2, 1))
    log_gap = cum_heads[:, :, :, None] - cum_heads[:, :, None, :]
    causal = jnp.arange(segment_len)[:, None] >= jnp.arange(segment_len)[None, :]
    weights = (
        jnp.where(causal, jnp.exp(jnp.where(causal, log_gap, 0.0)), 0.0) * step_heads[:, :, None, :]
    )
    mixing = (
        scores[:, :, None]
        * weights.reshape(segments, groups_here, group_heads, segment_len, segment_len)
    ).astype(jnp.bfloat16)
    x_heads = x_conv.reshape(segments, segment_len, groups_here, group_heads, head_dim)
    local_part = jnp.einsum(
        "cghls,csghp->clghp", mixing, x_heads, preferred_element_type=jnp.float32
    )
    tail_weight = jnp.exp(log_cum[:, -1:, :] - log_cum) * time_step
    x_weighted = (
        x_heads * tail_weight.reshape(segments, segment_len, groups_here, group_heads, 1)
    ).astype(jnp.bfloat16)
    block_state = jnp.einsum(
        "clghp,clgn->cghpn", x_weighted, b_mat, preferred_element_type=jnp.float32
    )
    block_decay = jnp.exp(log_cum[:, -1, :]).reshape(segments, groups_here, group_heads)
    running = jnp.zeros((groups_here, group_heads, head_dim, state_dim), jnp.float32)
    factor = jnp.ones((groups_here, group_heads), jnp.float32)
    starts = []
    factors = []
    for piece_index in range(segments):
        starts.append(running)
        factors.append(factor)
        running = block_decay[piece_index][..., None, None] * running + block_state[piece_index]
        factor = factor * block_decay[piece_index]
    is_first = lax.axis_index("seq") == 0
    seed_state = init_state.reshape(groups_here, group_heads, head_dim, state_dim)
    summary = running + jnp.where(is_first, factor[..., None, None] * seed_state, 0.0)
    source_count = lax.axis_size("seq")
    per_piece = heads_here // source_count
    flat_states = summary.reshape(source_count, per_piece, head_dim, state_dim)
    piece_decays = factor.reshape(source_count, per_piece)
    ordered = prefix_sources(
        (
            lax.all_to_all(piece_decays, "seq", split_axis=0, concat_axis=0, tiled=True),
            lax.all_to_all(flat_states, "seq", split_axis=0, concat_axis=0, tiled=True),
        )
    )
    prefix = lax.all_to_all(ordered, "seq", split_axis=0, concat_axis=0, tiled=True).reshape(
        groups_here, group_heads, head_dim, state_dim
    )
    incoming = prefix + jnp.where(is_first, seed_state, 0.0)
    start_states = jnp.stack(starts) + jnp.stack(factors)[..., None, None] * incoming
    state_low = start_states.astype(jnp.bfloat16)
    carried_part = jnp.exp(log_cum).reshape(
        segments, segment_len, groups_here, group_heads, 1
    ) * jnp.einsum("clgn,cghpn->clghp", c_mat, state_low, preferred_element_type=jnp.float32)
    skip_part = d_skip.reshape(groups_here, group_heads, 1) * x_heads
    mixed_out = (local_part + carried_part + skip_part).reshape(row_count, channels)
    gated_out = mixed_out * jax.nn.silu(z_gate.astype(jnp.float32))
    square_sum = jnp.sum(gated_out * gated_out, axis=1)
    total_square = lax.psum(square_sum, "head")
    inverse_rms = lax.rsqrt(total_square / INNER + norm_eps)
    return (gated_out * inverse_rms[:, None] * norm_gain).astype(jnp.bfloat16)


def solution(mesh):
    placed = (
        P("seq", "head"),
        P(None, "seq", "head"),
        P("seq", "head"),
        P("seq", "head"),
        P(None, "head"),
        P(None, None, "head"),
        P("head"),
        P("head"),
        P("head"),
        P("head", None, None),
        P("head"),
    )
    return jax.shard_map(
        local, mesh=mesh, in_specs=placed, out_specs=P("seq", "head"), check_vma=False
    )
```

profile of v0, /device:TPU:0, one launch (start us, length us, event | category | flops | bytes accessed | tf_op | source)
XLA Modules:
  0.0 324.5 jit_solution(15686120314785858558)
XLA Ops:
  0.0 0.7 slice.173
  0.7 4.9 %collective-permute-start.1 = (bf16[2,3,256]{2,1,0:T(4,128)(2,1)S(1)}, bf16[2,3,256]{2,1,0:T(4,128)(2,1)S(1)}, u32[]{:S(2)}, u32[]{:S(2)}) collective-permute-start(bf16[2,3,256]{2,1,0:T(4,128)(2,1)S(1)} %slice.173), channel_id=1, source_target_pairs={{0,1},{1,2},{2,3},{3,4},{4,5},{5,6},{6,7},{8,9},{9,10},{10,11},{11... | collective-permute-start | bytes 9224 | tf_op jit(solution)/shard_map/ppermute | solution.py:14
  5.6 0.9 slice.165
  6.4 3.4 %collective-permute-start = (bf16[3,4096]{1,0:T(4,128)(2,1)S(1)}, bf16[3,4096]{1,0:T(4,128)(2,1)S(1)}, u32[]{:S(2)}, u32[]{:S(2)}) collective-permute-start(bf16[3,4096]{1,0:T(4,128)(2,1)S(1)} %slice.165), channel_id=1, source_target_pairs={{0,1},{1,2},{2,3},{3,4},{4,5},{5,6},{6,7},{8,9},{9,10},{10,11},{11... | collective-permute-start | bytes 73736 | tf_op jit(solution)/shard_map/ppermute | solution.py:14
  9.9 1.0 compare_select_fusion
  10.9 0.7 exponential_negate_fusion
  11.9 2.3 reduce-window.6
  15.3 0.7 mul.461
  15.9 4.8 %all-to-all-start.1 = ((f32[8,1,4]{2,1,0:T(1,128)}), f32[8,1,4]{2,1,0:T(1,128)}, u32[]{:S(2)}, u32[]{:S(2)}) async-start(f32[8,1,4]{2,1,0:T(1,128)} %bitcast.18), calls=%async_computation.1 | async-start | bytes 8192 | tf_op jit(solution)/shard_map/all_to_all | solution.py:112
  20.8 0.9 fusion.46
  21.6 0.8 fusion.41
  22.4 1.1 fusion.45
  25.0 0.6 mul.432
  25.6 0.7 mul.435
  26.3 3.5 %multiply_convert_fusion.6 = bf16[2,1024,256]{2,1,0:T(8,128)(2,1)S(1)} fusion(bf16[2,1024,256]{2,1,0:T(8,128)(2,1)} %param.12, bf16[2,3,256]{2,1,0:T(4,128)(2,1)S(1)} %collective-permute-done.1, f32[2,256]{1,0:T(2,128)S(1)} %get-tuple-element.41, f32[2,256]{1,0:T(2,128)S(1)} %get-tuple-element.42, f32[2,256]{1,0:T(2,128)S(1)} %get-tuple-element.43, ...), kind=kLoop, calls=%fused_computation.41 | loop fusion | flops 13107200 | bytes 2108416 | tf_op jit(solution)/shard_map/convert_element_type | solution.py:63
  29.8 0.9 fusion.43
  30.8 18.9 %fusion.20 = bf16[128,8,32,128]{3,1,2,0:T(8,128)(2,1)} fusion(bf16[1024,4096]{1,0:T(8,128)(2,1)} %param.11, f32[4096]{0:T(1024)S(1)} %bitcast.98, bf16[3,4096]{1,0:T(4,128)(2,1)S(1)} %collective-permute-done, f32[4096]{0:T(1024)S(1)} %bitcast.99, f32[4096]{0:T(1024)S(1)} %bitcast.97, f32[4096]{0:T(1024)S(1)} %bitcast.96), kind=kLoop, calls=%fused_computation.32 | loop fusion | flops 104857600 | bytes 16867328
  49.8 9.4 %copy.115 = bf16[128,8,32,128]{3,2,1,0:T(8,128)(2,1)} copy(bf16[128,8,32,128]{3,1,2,0:T(8,128)(2,1)} %fusion.20) | data formatting | bytes 16777216
  59.2 13.7 %copy.89 = bf16[4,256,2,16,128]{1,4,3,2,0:T(8,128)(2,1)} copy(bf16[4,256,2,16,128]{4,3,2,1,0:T(8,128)(2,1)} %bitcast.83) | data formatting | bytes 16777216 | tf_op jit(solution)/shard_map/reshape | solution.py:82
  72.9 5.7 %fusion.16 = f32[4,2,16,128,128]{4,3,2,1,0:T(8,128)S(1)} fusion(bf16[4,256,2,16,128]{1,4,3,2,0:T(8,128)(2,1)} %copy.89, f32[4,256,2,16]{1,3,2,0:T(8,128)S(1)} %bitcast.94, bf16[4,256,2,128,1]{3,2,1,0,4:T(2,128)(2,1)S(1)} %bitcast.91), kind=kOutput, calls=%fused_computation.27 | convolution fusion | flops 1086324736 | bytes 17432576 | tf_op jit(solution)/shard_map/clghp,clgn->cghpn/dot_general | solution.py:90
  78.7 6.3 %multiply_add_fusion = (f32[1,2,16,128,128]{4,3,2,1,0:T(8,128)}, f32[1,2,16,128,128]{4,3,2,1,0:T(8,128)}, f32[1,2,16,128,128]{4,3,2,1,0:T(8,128)}, f32[1,2,16,12...) fusion(f32[2,16]{1,0:T(2,128)S(1)} %copy-done.13, ...), kind=kLoop, calls=%fused_computation.39 | loop fusion | flops 2621440 | bytes 23069056 | tf_op jit(solution)/shard_map/add | solution.py:101
  85.0 6.2 %select_add_fusion = f32[8,4,128,128]{3,2,1,0:T(8,128)} fusion(f32[8,4,128,128]{3,2,1,0:T(8,128)} %bitcast.89, f32[8,4,128,128]{3,2,1,0:T(8,128)} %bitcast.88, f32[8,4,128,128]{3,2,1,0:T(8,128)} %bitcast.87, f32[8,4,128,128]{3,2,1,0:T(8,128)} %bitcast.86, f32[8,4,128,128]{3,2,1,0:T(8,128)} %bitcast.85, f32[8,4]{1,0:T(8,128)S(1)} %copy-done.6, ...), kind=kLoop, calls=%fused_computation.38 | loop fusion | flops 5242880 | bytes 12583553 | tf_op jit(solution)/shard_map/add | solution.py:105
  91.3 6.0 %all-to-all-start = ((f32[8,4,128,128]{3,2,1,0:T(8,128)}), f32[8,4,128,128]{3,2,1,0:T(8,128)S(1)}, u32[]{:S(2)}, u32[]{:S(2)}) async-start(f32[8,4,128,128]{3,2,1,0:T(8,128)} %select_add_fusion), calls=%async_computation | async-start | bytes 4194304 | tf_op jit(solution)/shard_map/all_to_all | solution.py:113
  97.3 0.8 copy.95
  99.1 45.2 %all-to-all-done = f32[8,4,128,128]{3,2,1,0:T(8,128)S(1)} async-done(((f32[8,4,128,128]{3,2,1,0:T(8,128)}), f32[8,4,128,128]{3,2,1,0:T(8,128)S(1)}, u32[]{:S(2)}, u32[]{:S(2)}) %all-to-all-start) | async-done | bytes 2097184 | tf_op jit(solution)/shard_map/all_to_all | solution.py:113
  144.8 0.8 pad_add_fusion
  145.7 0.8 pad_maximum_fusion.3
  146.5 3.5 %pad.22 = f32[4,4,128,128]{3,2,1,0:T(8,128)S(1)} pad(f32[2,4,128,128]{3,2,1,0:T(8,128)} %pad_maximum_fusion.3, f32[]{:T(128)} %constant.9.clone.1), padding=0_1_1x0_0_0x0_0_0x0_0_0 | pad | bytes 1572868 | tf_op jit(solution)/shard_map/pad | solution.py:22
  150.0 5.7 %pad.23 = f32[4,4,128,128]{3,2,1,0:T(8,128)} pad(f32[2,4,128,128]{3,2,1,0:T(8,128)} %pad_add_fusion, f32[]{:T(128)} %constant.9.clone.1), padding=1_0_1x0_0_0x0_0_0x0_0_0 | pad | bytes 1572868 | tf_op jit(solution)/shard_map/pad | solution.py:22
  155.7 2.3 add.159
  158.1 10.1 %pad.114 = f32[8,4,128,128]{3,2,1,0:T(8,128)} pad(f32[4,4,128,128]{3,2,1,0:T(8,128)} %add.159, f32[]{:T(128)} %constant.9.clone.1), padding=1_0_1x0_0_0x0_0_0x0_0_0 | pad | bytes 3145732
  168.2 1.3 fusion.28
  169.9 1.7 slice_add_fusion.3
  171.6 1.6 concatenate.19
  173.2 4.4 %all-to-all-start.2 = ((f32[8,4,128,128]{3,2,1,0:T(8,128)}), f32[8,4,128,128]{3,2,1,0:T(8,128)}, u32[]{:S(2)}, u32[]{:S(2)}) async-start(f32[8,4,128,128]{3,2,1,0:T(8,128)} %concatenate.19), calls=%async_computation.2 | async-start | bytes 4194304 | tf_op jit(solution)/shard_map/all_to_all | solution.py:116
  178.3 0.6 iota_compare_fusion
  179.1 3.1 broadcast_select_fusion
  182.2 1.2 reshape_squeeze.6
  183.4 1.8 fusion.31
  185.2 40.2 %all-to-all-done.2 = f32[8,4,128,128]{3,2,1,0:T(8,128)} async-done(((f32[8,4,128,128]{3,2,1,0:T(8,128)}), f32[8,4,128,128]{3,2,1,0:T(8,128)}, u32[]{:S(2)}, u32[]{:S(2)}) %all-to-all-start.2) | async-done | bytes 2097184 | tf_op jit(solution)/shard_map/all_to_all | solution.py:116
  225.4 2.6 bitcast_add_fusion
  228.1 10.5 %fusion.21 = f32[4,2,16,128,256]{4,3,2,1,0:T(8,128)} fusion(f32[1,2,16,128,128]{4,3,2,1,0:T(8,128)S(1)} %copy-done, f32[1,2,16,128,128]{4,3,2,1,0:T(8,128)} %get-tuple-element.14, f32[1,2,16,128,128]{4,3,2,1,0:T(8,128)} %get-tuple-element.15, f32[4]{0:T(128)S(1)} %pad.35.clone, f32[2,16,128,128]{3,2,1,0:T(8,128)S(1)} %bitcast_add_fusion, ...), kind=kOutput, calls=%fused_computation.33 | convolution fusion | flops 1086324736 | bytes 25690640 | tf_op jit(solution)/shard_map/clgn,cghpn->clghp/dot_general | solution.py:124
  238.6 17.5 %fusion.2 = f32[4,256,2,16,128]{1,4,3,2,0:T(8,128)} fusion(bf16[4,256,2,16,128]{1,4,3,2,0:T(8,128)(2,1)S(1)} %bitcast.82, f32[4,2,16,128,256]{4,3,2,1,0:T(8,128)} %fusion.21, f32[4,2,16,256]{3,2,1,0:T(8,128)S(1)} %copy.88, f32[4,2,16,256]{3,2,1,0:T(8,128)S(1)} %reduce_window_sum.27, f32[4,2,256,256]{3,2,1,0:T(8,128)} %fusion.31, ...), kind=kOutput, calls=%fused_computation.7 | convolution fusion | flops 2218786816 | bytes 44499072 | tf_op jit(solution)/shard_map/cghls,csghp->clghp/dot_general | solution.py:83
  256.1 19.9 %copy.100 = f32[4,256,2,16,128]{4,3,2,1,0:T(8,128)} copy(f32[4,256,2,16,128]{1,4,3,2,0:T(8,128)} %fusion.2) | data formatting | bytes 33554432 | tf_op jit(solution)/shard_map/add | solution.py:126
  276.0 18.2 %reshape.230 = f32[1024,4096]{1,0:T(8,128)} reshape(f32[4,256,2,16,128]{4,3,2,1,0:T(8,128)} %copy.100) | data formatting | bytes 33554432 | tf_op jit(solution)/shard_map/reshape | solution.py:126
  294.2 10.7 %multiply_reduce_fusion = f32[1024]{0:T(1024)S(1)} fusion(f32[1024,4096]{1,0:T(8,128)} %reshape.230, bf16[1024,4096]{1,0:T(8,128)(2,1)} %param.14), kind=kLoop, calls=%fused_computation.15 | loop fusion | flops 33553408 | bytes 25169920 | tf_op jit(solution)/shard_map/reduce_sum | solution.py:128
  304.9 5.7 %psum.7 = f32[1024]{0:T(1024)S(1)} all-reduce(f32[1024]{0:T(1024)S(1)} %multiply_reduce_fusion), channel_id=1, replica_groups=mesh['head'=4,'seq'=8] {'head'}, use_global_device_ids=true, to_apply=%region_3.4 | all-reduce | flops 1024 | bytes 8192 | tf_op jit(solution)/shard_map/psum | solution.py:129
  310.6 13.9 %multiply_convert_fusion.2 = bf16[1024,4096]{1,0:T(8,128)(2,1)} fusion(f32[4096]{0:T(1024)S(1)} %copy-done.5, f32[1024]{0:T(1024)S(1)} %add_rsqrt_fusion, f32[1024,4096]{1,0:T(8,128)} %reshape.230, bf16[1024,4096]{1,0:T(8,128)(2,1)} %param.14), kind=kLoop, calls=%fused_computation.14 | loop fusion | flops 37748736 | bytes 33574912 | tf_op jit(solution)/shard_map/convert_element_type | solution.py:131
  (94 shorter events, 5.8 us)
Async XLA Ops:
  0.7 25.6 %collective-permute-start.1 = (bf16[2,3,256]{2,1,0:T(4,128)(2,1)S(1)}, bf16[2,3,256]{2,1,0:T(4,128)(2,1)S(1)}, u32[]{:S(2)}, u32[]{:S(2)}) collective-permute-start(bf16[2,3,256]{2,1,0:T(4,128)(2,1)S(1)} %slice.173), channel_id=1, source_target_pairs={{0,1},{1,2},{2,3},{3,4},{4,5},{5,6},{6,7},{8,9},{9,10},{10,11},{11... | collective-permute-start | bytes 9224 | tf_op jit(solution)/shard_map/ppermute | solution.py:14
  6.4 24.4 %collective-permute-start = (bf16[3,4096]{1,0:T(4,128)(2,1)S(1)}, bf16[3,4096]{1,0:T(4,128)(2,1)S(1)}, u32[]{:S(2)}, u32[]{:S(2)}) collective-permute-start(bf16[3,4096]{1,0:T(4,128)(2,1)S(1)} %slice.165), channel_id=1, source_target_pairs={{0,1},{1,2},{2,3},{3,4},{4,5},{5,6},{6,7},{8,9},{9,10},{10,11},{11... | collective-permute-start | bytes 73736 | tf_op jit(solution)/shard_map/ppermute | solution.py:14
  15.3 8.5 %copy-start.7 = (f32[32]{0:T(128)}, f32[32]{0:T(128)S(1)}, u32[]{:S(2)}) copy-start(f32[32]{0:T(128)S(1)} %get-tuple-element.40) | copy-start | bytes 388
  15.3 8.5 %copy-start.9 = (f32[32]{0:T(128)}, f32[32]{0:T(128)S(1)}, u32[]{:S(2)}) copy-start(f32[32]{0:T(128)S(1)} %get-tuple-element.38) | copy-start | bytes 388
  15.9 75.3 %all-to-all-start.1 = ((f32[8,1,4]{2,1,0:T(1,128)}), f32[8,1,4]{2,1,0:T(1,128)}, u32[]{:S(2)}, u32[]{:S(2)}) async-start(f32[8,1,4]{2,1,0:T(1,128)} %bitcast.18), calls=%async_computation.1 | async-start | bytes 8192 | tf_op jit(solution)/shard_map/all_to_all | solution.py:112
  30.8 42.1 %copy-start.1 = (bf16[4,256,2,128]{3,2,1,0:T(2,128)(2,1)}, bf16[4,256,2,128]{3,2,1,0:T(2,128)(2,1)S(1)}, u32[]{:S(2)}) copy-start(bf16[4,256,2,128]{3,2,1,0:T(2,128)(2,1)S(1)} %reshape_squeeze.7) | copy-start | bytes 1572868
  72.9 5.8 %copy-start.11 = (f32[2,16]{1,0:T(2,128)S(1)}, f32[2,16]{1,0:T(2,128)}, u32[]{:S(2)}) copy-start(f32[2,16]{1,0:T(2,128)} %mul.426) | copy-start | bytes 388
  72.9 5.8 %copy-start.12 = (f32[2,16]{1,0:T(2,128)S(1)}, f32[2,16]{1,0:T(2,128)}, u32[]{:S(2)}) copy-start(f32[2,16]{1,0:T(2,128)} %mul.432) | copy-start | bytes 388
  72.9 5.8 %copy-start.13 = (f32[2,16]{1,0:T(2,128)S(1)}, f32[2,16]{1,0:T(2,128)}, u32[]{:S(2)}) copy-start(f32[2,16]{1,0:T(2,128)} %mul.435) | copy-start | bytes 388
  78.7 6.4 %copy-start.6 = (f32[8,4]{1,0:T(8,128)S(1)}, f32[8,4]{1,0:T(8,128)}, u32[]{:S(2)}) copy-start(f32[8,4]{1,0:T(8,128)} %get-tuple-element.37) | copy-start | bytes 388
  91.3 53.1 %all-to-all-start = ((f32[8,4,128,128]{3,2,1,0:T(8,128)}), f32[8,4,128,128]{3,2,1,0:T(8,128)S(1)}, u32[]{:S(2)}, u32[]{:S(2)}) async-start(f32[8,4,128,128]{3,2,1,0:T(8,128)} %select_add_fusion), calls=%async_computation | async-start | bytes 4194304 | tf_op jit(solution)/shard_map/all_to_all | solution.py:113
  169.6 8.0 %copy-start.10 = (f32[32]{0:T(128)S(1)}, f32[32]{0:T(128)}, u32[]{:S(2)}) copy-start(f32[32]{0:T(128)} %copy-done.9) | copy-start | bytes 388
  169.6 8.1 %copy-start.8 = (f32[32]{0:T(128)S(1)}, f32[32]{0:T(128)}, u32[]{:S(2)}) copy-start(f32[32]{0:T(128)} %copy-done.7) | copy-start | bytes 388
  169.6 8.2 %copy-start.14 = (f32[32]{0:T(128)S(1)}, f32[32]{0:T(128)}, u32[]{:S(2)}) copy-start(f32[32]{0:T(128)} %get-tuple-element.5) | copy-start | bytes 388
  169.6 8.7 %copy-start.15 = (f32[32]{0:T(128)S(1)}, f32[32]{0:T(128)}, u32[]{:S(2)}) copy-start(f32[32]{0:T(128)} %param.19) | copy-start | bytes 388
  171.6 11.8 %copy-start.2 = (bf16[4,256,2,128]{3,2,1,0:T(2,128)(2,1)S(1)}, bf16[4,256,2,128]{3,2,1,0:T(2,128)(2,1)}, u32[]{:S(2)}) copy-start(bf16[4,256,2,128]{3,2,1,0:T(2,128)(2,1)} %copy-done.1) | copy-start | bytes 1572868
  173.2 52.2 %all-to-all-start.2 = ((f32[8,4,128,128]{3,2,1,0:T(8,128)}), f32[8,4,128,128]{3,2,1,0:T(8,128)}, u32[]{:S(2)}, u32[]{:S(2)}) async-start(f32[8,4,128,128]{3,2,1,0:T(8,128)} %concatenate.19), calls=%async_computation.2 | async-start | bytes 4194304 | tf_op jit(solution)/shard_map/all_to_all | solution.py:116
  177.6 50.4 %copy-start = (f32[1,2,16,128,128]{4,3,2,1,0:T(8,128)S(1)}, f32[1,2,16,128,128]{4,3,2,1,0:T(8,128)}, u32[]{:S(2)}) copy-start(f32[1,2,16,128,128]{4,3,2,1,0:T(8,128)} %get-tuple-element.13) | copy-start | bytes 6291460
  225.4 13.2 %slice-start = ((s8[8388608]{0:T(1024)(128)(4,1)}), s8[4194304]{0:T(1024)(128)(4,1)S(1)}, s32[]{:S(2)}) async-start(s8[8388608]{0:T(1024)(128)(4,1)} %bitcast.81), calls=%async_computation.3 | async-start | bytes 8388608
  228.0 10.5 %slice-start.1 = ((s8[8388608]{0:T(1024)(128)(4,1)}), s8[4194304]{0:T(1024)(128)(4,1)S(1)}, s32[]{:S(2)}) async-start(s8[8388608]{0:T(1024)(128)(4,1)} %bitcast.81), calls=%async_computation.4 | async-start | bytes 8388608
  228.0 10.5 %copy-start.3 = (f32[4,256,32]{1,2,0:T(8,128)S(1)}, f32[4,256,32]{1,2,0:T(8,128)}, u32[]{:S(2)}) copy-start(f32[4,256,32]{1,2,0:T(8,128)} %get-tuple-element.26) | copy-start | bytes 393220
  228.1 10.5 %copy-start.4 = (pred[256,256]{1,0:T(8,128)(4,1)S(1)}, pred[256,256]{1,0:T(8,128)(4,1)}, u32[]{:S(2)}) copy-start(pred[256,256]{1,0:T(8,128)(4,1)} %iota_compare_fusion) | copy-start | bytes 196612
  294.2 16.4 %copy-start.5 = (f32[4096]{0:T(1024)S(1)}, f32[4096]{0:T(1024)}, u32[]{:S(2)}) copy-start(f32[4096]{0:T(1024)} %param.21) | copy-start | bytes 49156
where the time goes:
time: 328 us; the launch traced here: 325 us
  local copies, waits for them, and re-layouts  94.1 us (29%)
  waiting for transfers between devices  85.5 us (26%)
  other arithmetic  79.9 us (24%)
  matrix products  35.5 us (11%)
  starting transfers between devices  23.5 us (7%)
  blocking collectives  5.67 us (2%)
    all_to_all x1, waiting for transfers between devices, local(): lax.all_to_all(flat_states, 'seq', split_axis=0, concat_axis=0, tiled=True)  45.2 us
    all_to_all x1, waiting for transfers between devices, local(): lax.all_to_all(ordered, 'seq', split_axis=0, concat_axis=0, tiled=True)  40.2 us
    add x1, local copies, waits for them, and re-layouts, local(): local_part + carried_part + skip_part  19.9 us
    unnamed x40, local copies, waits for them, and re-layouts  19.6 us
    unnamed x2, other arithmetic  18.9 us
    reshape x1, local copies, waits for them, and re-layouts, local(): (local_part + carried_part + skip_part).reshape(row_count, channels)  18.2 us
    dot_general x1, matrix products, local(): jnp.einsum('cghls,csghp->clghp', mixing, x_heads, preferred_element_type=...  17.5 us
    convert_element_type x1, other arithmetic, local(): return (gated_out * inverse_rms[:, None] * norm_gain).astype(jnp.bfloat16)  13.9 us
  transfers between devices with their start and end apart: 5, of which 2 were waited for; matrix products, arithmetic and copies ran while one was open for 27% of the time, Pallas kernels for 0%

commit v1 on v0

--- a/solution.py
+++ b/solution.py
@@ -6,6 +6,28 @@
 SPAN = 256
 INNER = 16384
 norm_eps = 1e-05
+
+
+def split_up(x, dim, count):
+    before, after = (x.shape[:dim], x.shape[dim + 1 :])
+    return jnp.moveaxis(x.reshape(*before, count, -1, *after), dim, 0)
+
+
+def joined_along(blocks, dim):
+    lengths = list(blocks.shape[1:])
+    lengths[dim] *= blocks.shape[0]
+    return jnp.moveaxis(blocks, 0, dim).reshape(lengths)
+
+
+def exchange_in_pairs(array, axis, split_dim, concat_dim):
+    count, mine = (lax.axis_size(axis), lax.axis_index(axis))
+    tiles = split_up(array, split_dim, count)
+    finished = [tiles[mine]]
+    for step in range(1, count):
+        sent = tiles[mine ^ step]
+        finished.append(lax.ppermute(sent, axis, [(i, i ^ step) for i in range(count)]))
+    tiles = jnp.stack(finished)[mine ^ jnp.arange(count)]
+    return joined_along(tiles, concat_dim)
 
 
 def from_behind(value, axis, by):
@@ -110,7 +132,7 @@
     ordered = prefix_sources(
         (
             lax.all_to_all(piece_decays, "seq", split_axis=0, concat_axis=0, tiled=True),
-            lax.all_to_all(flat_states, "seq", split_axis=0, concat_axis=0, tiled=True),
+            exchange_in_pairs(flat_states, "seq", 0, 0),
         )
     )
     prefix = lax.all_to_all(ordered, "seq", split_axis=0, concat_axis=0, tiled=True).reshape(

time: 328 us -> 333 us (1.015)
  waiting for transfers between devices: 85.5 us -> 66.7 us
  starting transfers between devices: 23.5 us -> 37.4 us
  local copies, waits for them, and re-layouts: 94.1 us -> 107 us
    all_to_all x1 -> x0, waiting for transfers between devices: 45.2 us -> none  [local(): lax.all_to_all(flat_states, 'seq', split_axis=0, concat_axis=0, tiled=True)]
    ppermute x0 -> x7, waiting for transfers between devices: none -> 28.8 us  [exchange_in_pairs(): lax.ppermute(sent, axis, [(i, i ^ step) for i in range(count)])]
    ppermute x0 -> x7, starting transfers between devices: none -> 12.5 us  [exchange_in_pairs(): lax.ppermute(sent, axis, [(i, i ^ step) for i in range(count)])]
    all_to_all x1, starting transfers between devices: 4.38 us -> 11.8 us  [local(): lax.all_to_all(ordered, 'seq', split_axis=0, concat_axis=0, tiled=True)]
    slice x1, local copies, waits for them, and re-layouts: 0.26 us -> 6.27 us  [prefix_sources(): inclusive[1][:-1]]
    all_to_all x1 -> x0, starting transfers between devices: 5.98 us -> none  [local(): lax.all_to_all(flat_states, 'seq', split_axis=0, concat_axis=0, tiled=True)]
    unnamed x40 -> x62, local copies, waits for them, and re-layouts: 19.6 us -> 24.5 us
  transfers between devices with their start and end apart: 5 -> 11, of which waited for: 2 -> 3; matrix products, arithmetic and copies ran while one was open for 27% -> 26% of each run, Pallas kernels for 0% -> 0%
where the time goes in v1:
time: 333 us; the launch traced here: 330 us
  local copies, waits for them, and re-layouts  107 us (32%)
  other arithmetic  77.2 us (23%)
  waiting for transfers between devices  66.7 us (20%)
  starting transfers between devices  37.4 us (11%)
  matrix products  35.6 us (11%)
  blocking collectives  5.67 us (2%)
    all_to_all x1, waiting for transfers between devices, local(): lax.all_to_all(ordered, 'seq', split_axis=0, concat_axis=0, tiled=True)  37.9 us
    ppermute x7, waiting for transfers between devices, exchange_in_pairs(): lax.ppermute(sent, axis, [(i, i ^ step) for i in range(count)])  28.8 us
    unnamed x62, local copies, waits for them, and re-layouts  24.5 us
    add x1, local copies, waits for them, and re-layouts, local(): local_part + carried_part + skip_part  19.9 us
    unnamed x2, other arithmetic  18.9 us
    reshape x1, local copies, waits for them, and re-layouts, local(): (local_part + carried_part + skip_part).reshape(row_count, channels)  18.2 us
    dot_general x1, matrix products, local(): jnp.einsum('cghls,csghp->clghp', mixing, x_heads, preferred_element_type=...  17.5 us
    convert_element_type x1, other arithmetic, local(): return (gated_out * inverse_rms[:, None] * norm_gain).astype(jnp.bfloat16)  13.9 us
  transfers between devices with their start and end apart: 11, of which 3 were waited for; matrix products, arithmetic and copies ran while one was open for 26% of the time, Pallas kernels for 0%

profile of v1, /device:TPU:0, one launch (start us, length us, event | category | flops | bytes accessed | tf_op | source)
XLA Modules:
  0.0 330.3 jit_solution(5911822677085195959)
XLA Ops:
  0.8 4.9 %collective-permute-start.1 = (bf16[2,3,256]{2,1,0:T(4,128)(2,1)S(1)}, bf16[2,3,256]{2,1,0:T(4,128)(2,1)S(1)}, u32[]{:S(2)}, u32[]{:S(2)}) collective-permute-start(bf16[2,3,256]{2,1,0:T(4,128)(2,1)S(1)} %slice.176), channel_id=1, source_target_pairs={{0,1},{1,2},{2,3},{3,4},{4,5},{5,6},{6,7},{8,9},{9,10},{10,11},{11... | collective-permute-start | bytes 9224 | tf_op jit(solution)/shard_map/ppermute | solution.py:36
  6.5 3.4 %collective-permute-start = (bf16[3,4096]{1,0:T(4,128)(2,1)S(1)}, bf16[3,4096]{1,0:T(4,128)(2,1)S(1)}, u32[]{:S(2)}, u32[]{:S(2)}) collective-permute-start(bf16[3,4096]{1,0:T(4,128)(2,1)S(1)} %slice.168), channel_id=1, source_target_pairs={{0,1},{1,2},{2,3},{3,4},{4,5},{5,6},{6,7},{8,9},{9,10},{10,11},{11... | collective-permute-start | bytes 73736 | tf_op jit(solution)/shard_map/ppermute | solution.py:36
  10.0 1.0 compare_select_fusion
  12.0 2.3 reduce-window.6
  16.0 4.8 %all-to-all-start = ((f32[8,1,4]{2,1,0:T(1,128)}), f32[8,1,4]{2,1,0:T(1,128)}, u32[]{:S(2)}, u32[]{:S(2)}) async-start(f32[8,1,4]{2,1,0:T(1,128)} %bitcast.34), calls=%async_computation | async-start | bytes 8192 | tf_op jit(solution)/shard_map/all_to_all | solution.py:134
  25.0 1.5 multiply_convert_fusion.6
  26.5 0.9 fusion.44
  27.5 18.9 %fusion.20 = bf16[128,8,32,128]{3,1,2,0:T(8,128)(2,1)} fusion(bf16[1024,4096]{1,0:T(8,128)(2,1)} %param.11, f32[4096]{0:T(1024)S(1)} %bitcast.131, bf16[3,4096]{1,0:T(4,128)(2,1)S(1)} %collective-permute-done, f32[4096]{0:T(1024)S(1)} %bitcast.132, f32[4096]{0:T(1024)S(1)} %bitcast.130, f32[4096]{0:T(1024)S(1)} %bitcast.129), kind=kLoop, calls=%fused_computation.33 | loop fusion | flops 104857600 | bytes 16867328
  46.5 9.4 %copy.115 = bf16[128,8,32,128]{3,2,1,0:T(8,128)(2,1)} copy(bf16[128,8,32,128]{3,1,2,0:T(8,128)(2,1)} %fusion.20) | data formatting | bytes 16777216
  55.9 13.7 %copy.89 = bf16[4,256,2,16,128]{1,4,3,2,0:T(8,128)(2,1)} copy(bf16[4,256,2,16,128]{4,3,2,1,0:T(8,128)(2,1)} %bitcast.114) | data formatting | bytes 16777216 | tf_op jit(solution)/shard_map/reshape | solution.py:104
  69.6 5.7 %fusion.16 = f32[4,2,16,128,128]{4,3,2,1,0:T(8,128)S(1)} fusion(bf16[4,256,2,16,128]{1,4,3,2,0:T(8,128)(2,1)} %copy.89, f32[4,256,2,16]{1,3,2,0:T(8,128)S(1)} %bitcast.127, bf16[4,256,2,128,1]{3,2,1,0,4:T(2,128)(2,1)S(1)} %bitcast.123), kind=kOutput, calls=%fused_computation.28 | convolution fusion | flops 1086324736 | bytes 17432576 | tf_op jit(solution)/shard_map/clghp,clgn->cghpn/dot_general | solution.py:112
  75.4 6.3 %multiply_add_fusion = (f32[1,2,16,128,128]{4,3,2,1,0:T(8,128)}, f32[1,2,16,128,128]{4,3,2,1,0:T(8,128)}, f32[1,2,16,128,128]{4,3,2,1,0:T(8,128)}, f32[1,2,16,12...) fusion(f32[2,16]{1,0:T(2,128)S(1)} %copy-done.20, ...), kind=kLoop, calls=%fused_computation.40 | loop fusion | flops 2621440 | bytes 23069056 | tf_op jit(solution)/shard_map/add | solution.py:123
  81.7 4.9 %select_add_fusion = f32[8,1,4,128,128]{4,3,2,0,1:T(8,128)S(1)} fusion(f32[8,1,4,128,128]{4,3,2,0,1:T(8,128)} %bitcast.121, f32[8,1,4,128,128]{4,3,2,0,1:T(8,128)} %bitcast.120, f32[8,1,4,128,128]{4,3,2,0,1:T(8,128)} %bitcast.119, f32[8,1,4,128,128]{4,3,2,0,1:T(8,128)} %bitcast.118, f32[8,1,4,128,128]{4,3,2,0,1:T(8,128)} %bitcast.117, ...), kind=kLoop, calls=%fused_computation.39 | loop fusion | flops 5242880 | bytes 12583553 | tf_op jit(solution)/shard_map/add | solution.py:127
  86.7 1.0 dynamic-slice_bitcast_fusion
  87.7 2.0 collective-permute-start.2
  91.1 1.5 collective-permute-start.3
  93.2 2.9 collective-permute-start.5
  96.1 1.4 collective-permute-start.6
  97.5 3.3 collective-permute-start.7
  100.8 1.0 bitcast_dynamic-update-slice_fusion.6
  101.8 8.6 %collective-permute-done.3 = f32[1,4,128,128]{3,2,1,0:T(8,128)} collective-permute-done((f32[1,4,128,128]{3,2,1,0:T(8,128)}, f32[1,4,128,128]{3,2,1,0:T(8,128)}, u32[]{:S(2)}, u32[]{:S(2)}) %collective-permute-start.3) | collective-permute-done | bytes 262176 | tf_op jit(solution)/shard_map/ppermute | solution.py:28
  110.3 1.3 collective-permute-start.8
  111.6 1.0 bitcast_dynamic-update-slice_fusion.5
  112.6 20.2 %collective-permute-done.6 = f32[1,4,128,128]{3,2,1,0:T(8,128)S(1)} collective-permute-done((f32[1,4,128,128]{3,2,1,0:T(8,128)S(1)}, f32[1,4,128,128]{3,2,1,0:T(8,128)S(1)}, u32[]{:S(2)}, u32[]{:S(2)}) %collective-permute-start.6) | collective-permute-done | bytes 262176 | tf_op jit(solution)/shard_map/ppermute | solution.py:28
  132.9 1.3 copy-done.5
  134.3 2.3 gather_fusion
  139.4 3.5 %pad.22 = f32[4,4,128,128]{3,2,1,0:T(8,128)S(1)} pad(f32[2,4,128,128]{3,2,1,0:T(8,128)} %pad_maximum_fusion.3, f32[]{:T(128)} %constant.15.clone.1), padding=0_1_1x0_0_0x0_0_0x0_0_0 | pad | bytes 1572868 | tf_op jit(solution)/shard_map/pad | solution.py:44
  142.9 5.7 %pad.23 = f32[4,4,128,128]{3,2,1,0:T(8,128)} pad(f32[2,4,128,128]{3,2,1,0:T(8,128)} %pad_add_fusion, f32[]{:T(128)} %constant.15.clone.1), padding=1_0_1x0_0_0x0_0_0x0_0_0 | pad | bytes 1572868 | tf_op jit(solution)/shard_map/pad | solution.py:44
  148.6 2.3 add.232
  151.0 10.1 %pad.116 = f32[8,4,128,128]{3,2,1,0:T(8,128)} pad(f32[4,4,128,128]{3,2,1,0:T(8,128)} %add.232, f32[]{:T(128)} %constant.15.clone.1), padding=1_0_1x0_0_0x0_0_0x0_0_0 | pad | bytes 3145732
  161.1 1.3 fusion.28
  162.5 6.3 %pad.48 = f32[7,4,128,128]{3,2,1,0:T(8,128)} pad(f32[4,4,128,128]{3,2,1,0:T(8,128)S(1)} %pad_maximum_fusion.2, f32[]{:T(128)} %constant.15.clone.1), padding=0_0_1x0_0_0x0_0_0x0_0_0 | pad | bytes 2883588 | tf_op jit(solution)/shard_map/slice | solution.py:45
  168.8 1.7 slice_add_fusion.3
  170.5 1.6 concatenate.19
  172.2 11.8 %all-to-all-start.1 = ((f32[8,4,128,128]{3,2,1,0:T(8,128)}), f32[8,4,128,128]{3,2,1,0:T(8,128)S(1)}, u32[]{:S(2)}, u32[]{:S(2)}) async-start(f32[8,4,128,128]{3,2,1,0:T(8,128)} %concatenate.19), calls=%async_computation.1 | async-start | bytes 4194304 | tf_op jit(solution)/shard_map/all_to_all | solution.py:138
  185.4 3.2 broadcast_select_fusion
  188.7 1.2 reshape_squeeze.6
  189.8 1.8 fusion.31
  191.6 37.9 %all-to-all-done.1 = f32[8,4,128,128]{3,2,1,0:T(8,128)S(1)} async-done(((f32[8,4,128,128]{3,2,1,0:T(8,128)}), f32[8,4,128,128]{3,2,1,0:T(8,128)S(1)}, u32[]{:S(2)}, u32[]{:S(2)}) %all-to-all-start.1) | async-done | bytes 2097184 | tf_op jit(solution)/shard_map/all_to_all | solution.py:138
  229.5 1.3 copy-done.1
  230.8 2.6 bitcast_add_fusion
  233.7 10.6 %fusion.21 = f32[4,2,16,128,256]{4,3,2,1,0:T(8,128)} fusion(f32[1,2,16,128,128]{4,3,2,1,0:T(8,128)S(1)} %copy-done, f32[1,2,16,128,128]{4,3,2,1,0:T(8,128)} %get-tuple-element.14, f32[1,2,16,128,128]{4,3,2,1,0:T(8,128)} %get-tuple-element.15, f32[4]{0:T(128)S(1)} %pad.35.clone, f32[2,16,128,128]{3,2,1,0:T(8,128)S(1)} %bitcast_add_fusion, ...), kind=kOutput, calls=%fused_computation.34 | convolution fusion | flops 1086324736 | bytes 25690640 | tf_op jit(solution)/shard_map/clgn,cghpn->clghp/dot_general | solution.py:146
  244.3 17.5 %fusion.2 = f32[4,256,2,16,128]{1,4,3,2,0:T(8,128)} fusion(bf16[4,256,2,16,128]{1,4,3,2,0:T(8,128)(2,1)S(1)} %bitcast.113, f32[4,2,16,128,256]{4,3,2,1,0:T(8,128)} %fusion.21, f32[4,2,16,256]{3,2,1,0:T(8,128)S(1)} %copy.88, f32[4,2,16,256]{3,2,1,0:T(8,128)S(1)} %reduce_window_sum.27, f32[4,2,256,256]{3,2,1,0:T(8,128)} %fusion.31, ...), kind=kOutput, calls=%fused_computation.8 | convolution fusion | flops 2218786816 | bytes 44499072 | tf_op jit(solution)/shard_map/cghls,csghp->clghp/dot_general | solution.py:105
  261.8 19.9 %copy.100 = f32[4,256,2,16,128]{4,3,2,1,0:T(8,128)} copy(f32[4,256,2,16,128]{1,4,3,2,0:T(8,128)} %fusion.2) | data formatting | bytes 33554432 | tf_op jit(solution)/shard_map/add | solution.py:148
  281.7 18.2 %reshape.320 = f32[1024,4096]{1,0:T(8,128)} reshape(f32[4,256,2,16,128]{4,3,2,1,0:T(8,128)} %copy.100) | data formatting | bytes 33554432 | tf_op jit(solution)/shard_map/reshape | solution.py:148
  299.9 10.7 %multiply_reduce_fusion = f32[1024]{0:T(1024)S(1)} fusion(f32[1024,4096]{1,0:T(8,128)} %reshape.320, bf16[1024,4096]{1,0:T(8,128)(2,1)} %param.14), kind=kLoop, calls=%fused_computation.16 | loop fusion | flops 33553408 | bytes 25169920 | tf_op jit(solution)/shard_map/reduce_sum | solution.py:150
  310.7 5.7 %psum.7 = f32[1024]{0:T(1024)S(1)} all-reduce(f32[1024]{0:T(1024)S(1)} %multiply_reduce_fusion), channel_id=1, replica_groups=mesh['head'=4,'seq'=8] {'head'}, use_global_device_ids=true, to_apply=%region_3.4 | all-reduce | flops 1024 | bytes 8192 | tf_op jit(solution)/shard_map/psum | solution.py:151
  316.4 13.9 %multiply_convert_fusion.2 = bf16[1024,4096]{1,0:T(8,128)(2,1)} fusion(f32[4096]{0:T(1024)S(1)} %copy-done.11, f32[1024]{0:T(1024)S(1)} %add_rsqrt_fusion, f32[1024,4096]{1,0:T(8,128)} %reshape.320, bf16[1024,4096]{1,0:T(8,128)(2,1)} %param.14), kind=kLoop, calls=%fused_computation.15 | loop fusion | flops 37748736 | bytes 33574912 | tf_op jit(solution)/shard_map/convert_element_type | solution.py:153
  (133 shorter events, 15.3 us)
Async XLA Ops:
  0.0 25.0 %copy-start.6 = (bf16[2,1024,256]{2,1,0:T(8,128)(2,1)S(1)}, bf16[2,1024,256]{2,1,0:T(8,128)(2,1)}, u32[]{:S(2)}) copy-start(bf16[2,1024,256]{2,1,0:T(8,128)(2,1)} %param.12) | copy-start | bytes 3145732
  0.0 20.8 %copy-start.13 = (f32[2,4,256]{2,1,0:T(4,128)S(1)}, f32[2,4,256]{2,1,0:T(4,128)}, u32[]{:S(2)}) copy-start(f32[2,4,256]{2,1,0:T(4,128)} %param.16) | copy-start | bytes 24580
  0.0 21.6 %copy-start.9 = (f32[4,4096]{1,0:T(4,128)S(1)}, f32[4,4096]{1,0:T(4,128)}, u32[]{:S(2)}) copy-start(f32[4,4096]{1,0:T(4,128)} %param.15) | copy-start | bytes 196612
  0.8 24.2 %collective-permute-start.1 = (bf16[2,3,256]{2,1,0:T(4,128)(2,1)S(1)}, bf16[2,3,256]{2,1,0:T(4,128)(2,1)S(1)}, u32[]{:S(2)}, u32[]{:S(2)}) collective-permute-start(bf16[2,3,256]{2,1,0:T(4,128)(2,1)S(1)} %slice.176), channel_id=1, source_target_pairs={{0,1},{1,2},{2,3},{3,4},{4,5},{5,6},{6,7},{8,9},{9,10},{10,11},{11... | collective-permute-start | bytes 9224 | tf_op jit(solution)/shard_map/ppermute | solution.py:36
  6.5 21.0 %collective-permute-start = (bf16[3,4096]{1,0:T(4,128)(2,1)S(1)}, bf16[3,4096]{1,0:T(4,128)(2,1)S(1)}, u32[]{:S(2)}, u32[]{:S(2)}) collective-permute-start(bf16[3,4096]{1,0:T(4,128)(2,1)S(1)} %slice.168), channel_id=1, source_target_pairs={{0,1},{1,2},{2,3},{3,4},{4,5},{5,6},{6,7},{8,9},{9,10},{10,11},{11... | collective-permute-start | bytes 73736 | tf_op jit(solution)/shard_map/ppermute | solution.py:36
  15.3 12.1 %copy-start.14 = (f32[32]{0:T(128)}, f32[32]{0:T(128)S(1)}, u32[]{:S(2)}) copy-start(f32[32]{0:T(128)S(1)} %get-tuple-element.48) | copy-start | bytes 388
  15.3 12.1 %copy-start.16 = (f32[32]{0:T(128)}, f32[32]{0:T(128)S(1)}, u32[]{:S(2)}) copy-start(f32[32]{0:T(128)S(1)} %get-tuple-element.46) | copy-start | bytes 388
  16.0 73.7 %all-to-all-start = ((f32[8,1,4]{2,1,0:T(1,128)}), f32[8,1,4]{2,1,0:T(1,128)}, u32[]{:S(2)}, u32[]{:S(2)}) async-start(f32[8,1,4]{2,1,0:T(1,128)} %bitcast.34), calls=%async_computation | async-start | bytes 8192 | tf_op jit(solution)/shard_map/all_to_all | solution.py:134
  27.5 42.1 %copy-start.3 = (bf16[4,256,2,128]{3,2,1,0:T(2,128)(2,1)}, bf16[4,256,2,128]{3,2,1,0:T(2,128)(2,1)S(1)}, u32[]{:S(2)}) copy-start(bf16[4,256,2,128]{3,2,1,0:T(2,128)(2,1)S(1)} %reshape_squeeze.7) | copy-start | bytes 1572868
  69.6 5.8 %copy-start.18 = (f32[2,16]{1,0:T(2,128)S(1)}, f32[2,16]{1,0:T(2,128)}, u32[]{:S(2)}) copy-start(f32[2,16]{1,0:T(2,128)} %mul.450) | copy-start | bytes 388
  69.6 5.8 %copy-start.19 = (f32[2,16]{1,0:T(2,128)S(1)}, f32[2,16]{1,0:T(2,128)}, u32[]{:S(2)}) copy-start(f32[2,16]{1,0:T(2,128)} %mul.456) | copy-start | bytes 388
  69.6 5.8 %copy-start.20 = (f32[2,16]{1,0:T(2,128)S(1)}, f32[2,16]{1,0:T(2,128)}, u32[]{:S(2)}) copy-start(f32[2,16]{1,0:T(2,128)} %mul.459) | copy-start | bytes 388
  75.4 6.4 %copy-start.12 = (f32[8,4]{1,0:T(8,128)S(1)}, f32[8,4]{1,0:T(8,128)}, u32[]{:S(2)}) copy-start(f32[8,4]{1,0:T(8,128)} %get-tuple-element.45) | copy-start | bytes 388
  86.7 3.0 copy-start.21
  87.7 9.8 %collective-permute-start.2 = (f32[1,4,128,128]{3,2,1,0:T(8,128)}, f32[1,4,128,128]{3,2,1,0:T(8,128)}, u32[]{:S(2)}, u32[]{:S(2)}) collective-permute-start(f32[1,4,128,128]{3,2,1,0:T(8,128)} %get-tuple-element.26), channel_id=1, source_target_pairs={{0,1},{1,0},{2,3},{3,2},{4,5},{5,4},{6,7},{7,6},{8,9},{9,8},{10,11... | collective-permute-start | bytes 786440 | tf_op jit(solution)/shard_map/ppermute | solution.py:28
  91.1 19.3 %collective-permute-start.3 = (f32[1,4,128,128]{3,2,1,0:T(8,128)}, f32[1,4,128,128]{3,2,1,0:T(8,128)}, u32[]{:S(2)}, u32[]{:S(2)}) collective-permute-start(f32[1,4,128,128]{3,2,1,0:T(8,128)} %get-tuple-element.25), channel_id=1, source_target_pairs={{0,2},{1,3},{2,0},{3,1},{4,6},{5,7},{6,4},{7,5},{8,10},{9,11},{10,... | collective-permute-start | bytes 786440 | tf_op jit(solution)/shard_map/ppermute | solution.py:28
  93.2 19.4 %collective-permute-start.4 = (f32[1,4,128,128]{3,2,1,0:T(8,128)}, f32[1,4,128,128]{3,2,1,0:T(8,128)S(1)}, u32[]{:S(2)}, u32[]{:S(2)}) collective-permute-start(f32[1,4,128,128]{3,2,1,0:T(8,128)} %get-tuple-element.24), channel_id=1, source_target_pairs={{0,3},{1,2},{2,1},{3,0},{4,7},{5,6},{6,5},{7,4},{8,11},{9,10},{10,... | collective-permute-start | bytes 786440 | tf_op jit(solution)/shard_map/ppermute | solution.py:28
  93.2 19.4 %collective-permute-start.5 = (f32[1,4,128,128]{3,2,1,0:T(8,128)S(1)}, f32[1,4,128,128]{3,2,1,0:T(8,128)S(1)}, u32[]{:S(2)}, u32[]{:S(2)}) collective-permute-start(f32[1,4,128,128]{3,2,1,0:T(8,128)S(1)} %get-tuple-element.23), channel_id=1, source_target_pairs={{0,4},{1,5},{2,6},{3,7},{4,0},{5,1},{6,2},{7,3},{8,12},{9,13},{10,... | collective-permute-start | bytes 786440 | tf_op jit(solution)/shard_map/ppermute | solution.py:28
  96.1 36.8 %collective-permute-start.6 = (f32[1,4,128,128]{3,2,1,0:T(8,128)S(1)}, f32[1,4,128,128]{3,2,1,0:T(8,128)S(1)}, u32[]{:S(2)}, u32[]{:S(2)}) collective-permute-start(f32[1,4,128,128]{3,2,1,0:T(8,128)S(1)} %get-tuple-element.22), channel_id=1, source_target_pairs={{0,5},{1,4},{2,7},{3,6},{4,1},{5,0},{6,3},{7,2},{8,13},{9,12},{10,... | collective-permute-start | bytes 786440 | tf_op jit(solution)/shard_map/ppermute | solution.py:28
  97.5 35.3 %collective-permute-start.7 = (f32[1,4,128,128]{3,2,1,0:T(8,128)S(1)}, f32[1,4,128,128]{3,2,1,0:T(8,128)S(1)}, u32[]{:S(2)}, u32[]{:S(2)}) collective-permute-start(f32[1,4,128,128]{3,2,1,0:T(8,128)S(1)} %get-tuple-element.21), channel_id=1, source_target_pairs={{0,6},{1,7},{2,4},{3,5},{4,2},{5,3},{6,0},{7,1},{8,14},{9,15},{10,... | collective-permute-start | bytes 786440 | tf_op jit(solution)/shard_map/ppermute | solution.py:28
  110.3 22.6 %collective-permute-start.8 = (f32[1,4,128,128]{3,2,1,0:T(8,128)S(1)}, f32[1,4,128,128]{3,2,1,0:T(8,128)S(1)}, u32[]{:S(2)}, u32[]{:S(2)}) collective-permute-start(f32[1,4,128,128]{3,2,1,0:T(8,128)S(1)} %get-tuple-element.20), channel_id=1, source_target_pairs={{0,7},{1,6},{2,5},{3,4},{4,3},{5,2},{6,1},{7,0},{8,15},{9,14},{10,... | collective-permute-start | bytes 786440 | tf_op jit(solution)/shard_map/ppermute | solution.py:28
  132.9 1.3 copy-start.5
  161.1 1.3 copy-start.7
  162.4 6.4 %copy-start.2 = (f32[8,4,128,128]{3,2,1,0:T(8,128)S(1)}, f32[8,4,128,128]{3,2,1,0:T(8,128)}, u32[]{:S(2)}) copy-start(f32[8,4,128,128]{3,2,1,0:T(8,128)} %pad.116) | copy-start | bytes 6291460
  172.1 11.9 %copy-start.17 = (f32[32]{0:T(128)S(1)}, f32[32]{0:T(128)}, u32[]{:S(2)}) copy-start(f32[32]{0:T(128)} %copy-done.16) | copy-start | bytes 388
  172.1 11.9 %copy-start.15 = (f32[32]{0:T(128)S(1)}, f32[32]{0:T(128)}, u32[]{:S(2)}) copy-start(f32[32]{0:T(128)} %copy-done.14) | copy-start | bytes 388
  172.1 12.0 %copy-start.22 = (f32[32]{0:T(128)S(1)}, f32[32]{0:T(128)}, u32[]{:S(2)}) copy-start(f32[32]{0:T(128)} %get-tuple-element.5) | copy-start | bytes 388
  172.1 12.5 %copy-start.23 = (f32[32]{0:T(128)S(1)}, f32[32]{0:T(128)}, u32[]{:S(2)}) copy-start(f32[32]{0:T(128)} %param.19) | copy-start | bytes 388
  172.2 57.4 %all-to-all-start.1 = ((f32[8,4,128,128]{3,2,1,0:T(8,128)}), f32[8,4,128,128]{3,2,1,0:T(8,128)S(1)}, u32[]{:S(2)}, u32[]{:S(2)}) async-start(f32[8,4,128,128]{3,2,1,0:T(8,128)} %concatenate.19), calls=%async_computation.1 | async-start | bytes 4194304 | tf_op jit(solution)/shard_map/all_to_all | solution.py:138
  185.4 4.4 %copy-start.4 = (bf16[4,256,2,128]{3,2,1,0:T(2,128)(2,1)S(1)}, bf16[4,256,2,128]{3,2,1,0:T(2,128)(2,1)}, u32[]{:S(2)}) copy-start(bf16[4,256,2,128]{3,2,1,0:T(2,128)(2,1)} %copy-done.3) | copy-start | bytes 1572868
  229.5 1.3 copy-start.1
  230.8 2.9 copy-start
  230.8 13.5 %slice-start = ((s8[8388608]{0:T(1024)(128)(4,1)}), s8[4194304]{0:T(1024)(128)(4,1)S(1)}, s32[]{:S(2)}) async-start(s8[8388608]{0:T(1024)(128)(4,1)} %bitcast.112), calls=%async_computation.2 | async-start | bytes 8388608
  233.7 10.6 %slice-start.1 = ((s8[8388608]{0:T(1024)(128)(4,1)}), s8[4194304]{0:T(1024)(128)(4,1)S(1)}, s32[]{:S(2)}) async-start(s8[8388608]{0:T(1024)(128)(4,1)} %bitcast.112), calls=%async_computation.3 | async-start | bytes 8388608
  233.7 10.6 %copy-start.8 = (f32[4,256,32]{1,2,0:T(8,128)S(1)}, f32[4,256,32]{1,2,0:T(8,128)}, u32[]{:S(2)}) copy-start(f32[4,256,32]{1,2,0:T(8,128)} %get-tuple-element.34) | copy-start | bytes 393220
  233.7 10.6 %copy-start.10 = (pred[256,256]{1,0:T(8,128)(4,1)S(1)}, pred[256,256]{1,0:T(8,128)(4,1)}, u32[]{:S(2)}) copy-start(pred[256,256]{1,0:T(8,128)(4,1)} %iota_compare_fusion) | copy-start | bytes 196612
  299.9 16.4 %copy-start.11 = (f32[4096]{0:T(1024)S(1)}, f32[4096]{0:T(1024)}, u32[]{:S(2)}) copy-start(f32[4096]{0:T(1024)} %param.21) | copy-start | bytes 49156
